TPU v7x, 32 devices: a whole 2x2x4 slice. The times are simulated.
32 devices in a mesh: pb: 8 (over z, x), vert: 4 (over y, core).
Axes of the slice: x: 2, y: 2, z: 4, core: 2. Of those that a mesh axis runs over, the one named last changes fastest.
Arguments:
- orbitals: bfloat16 [16, 32, 1024], P('pb', None, 'vert'), may hold values from -6 to 6
- transition: float32 [16, 256], P('pb'), may hold values from -0.9 to 0.9
- trial: float32 [8, 16, 256], P('vert', 'pb'), may hold values from -6 to 6
- screened: bfloat16 [16, 1024, 1024], P('pb', None, 'vert'), may hold values from -0.00030517578 to 0.00030517578
- bare: bfloat16 [1024, 1024], replicated, may hold values from -6.1035156e-05 to 6.1035156e-05
- cheb: float32 [3], replicated, may hold values from 0.5 to 1.5
- pair_k: int32 [24], P('pb'), may hold values from 0 to 15
- pair_slot: int32 [24], P('pb'), may hold values from 0 to 1
- k_order: int32 [16], replicated, may hold values from 0 to 15, each once
Outputs:
- filtered: float32 [8, 16, 256], P('vert', 'pb')
Inputs may be any that keep to these rules, and one draw needn't show every extreme that they name: The pair i lies with the owner of its momentum transfer 2 * (i // 3) + pair_slot[i]. `k_order`: A permutation of the k-points.
All inputs are finite; a program needn't handle non-finite values.
Results may differ from a plain program's by a relative error of at most 0.0075.
Values may be sent and summed in bfloat16 or wider, within the bound.
A program may use at most 64 MiB of HBM per device.

v0:
```python
import jax
import jax.numpy as jnp
from jax import lax
from jax.sharding import PartitionSpec as P

NV = 16


def body(orbitals, transition, trial, screened, bare, cheb, pair_k, pair_slot, k_order):
    kpoint_local = orbitals.shape[0]
    band_all = orbitals.shape[1]
    point_local = orbitals.shape[2]
    pair_count = pair_k.shape[0]
    kpoint_total = k_order.shape[0]
    valence = NV
    conduction = band_all - valence
    pair_width = valence * conduction
    end_count = 2 * pair_count
    hp = lax.Precision.HIGHEST
    position = lax.axis_index("pb")
    momentum = position * kpoint_local + pair_slot
    partner = jnp.mod(pair_k - momentum, kpoint_total)
    pair_ends = jnp.stack([pair_k, partner], axis=1).reshape(-1)
    owner_rows = jnp.arange(kpoint_total, dtype=jnp.int32)
    destination = jnp.sum(
        jnp.where(pair_ends[:, None] == k_order[None, :], owner_rows[None, :], 0), axis=1
    )
    shard_piece = lax.all_gather(orbitals, "pb", axis=0, tiled=True)
    row_count = shard_piece.shape[0]
    onehot = (destination[:, None] == jnp.arange(row_count, dtype=jnp.int32)[None, :]).astype(
        jnp.bfloat16
    )
    picked = jnp.dot(onehot, shard_piece.reshape(row_count, -1), preferred_element_type=jnp.float32)
    picked = picked.astype(jnp.bfloat16).reshape(end_count, band_all, point_local)
    val_points = lax.all_gather(picked[:, :valence, :], "vert", axis=2, tiled=True)
    point_total = val_points.shape[2]
    val_pairs = val_points.reshape(pair_count, 2, valence, point_total)
    cond_pairs = picked[:, valence:, :].reshape(pair_count, 2, conduction, point_local)

    def build_block(pair_index):
        val_both = val_pairs[pair_index].astype(jnp.float32)
        cond_both = cond_pairs[pair_index].astype(jnp.float32)
        left_pair = (
            (val_both[0][:, None, :] * val_both[1][None, :, :])
            .reshape(valence * valence, point_total)
            .astype(jnp.bfloat16)
        )
        right_pair = (
            (cond_both[0][:, None, :] * cond_both[1][None, :, :])
            .reshape(conduction * conduction, point_local)
            .astype(jnp.bfloat16)
        )
        matrix = screened[pair_slot[pair_index]]
        half_product = jnp.dot(left_pair, matrix, preferred_element_type=jnp.float32).astype(
            jnp.bfloat16
        )
        block_part = lax.dot_general(
            half_product, right_pair, (((1,), (1,)), ((), ())), preferred_element_type=jnp.float32
        )
        return (
            block_part.reshape(valence, valence, conduction, conduction)
            .transpose(0, 2, 1, 3)
            .reshape(pair_width, pair_width)
        )

    block_parts = lax.map(build_block, jnp.arange(pair_count, dtype=jnp.int32))
    blocks = lax.psum(block_parts, "vert")
    gathered_own = lax.all_gather(orbitals, "vert", axis=2, tiled=True).astype(jnp.float32)
    products = (
        (gathered_own[:, :valence, None, :] * gathered_own[:, None, valence:, :])
        .reshape(kpoint_local, pair_width, point_total)
        .astype(jnp.bfloat16)
    )

    def pick_trial(shard_piece):
        row_count = shard_piece.shape[1]
        onehot = (destination[:, None] == jnp.arange(row_count, dtype=jnp.int32)[None, :]).astype(
            jnp.bfloat16
        )
        return jnp.einsum("er,nrj->nej", onehot, shard_piece, preferred_element_type=jnp.float32)

    def apply_kernel(current):
        fetched = pick_trial(lax.all_gather(current, "pb", axis=1, tiled=True)).astype(jnp.bfloat16)
        pair_view = fetched.astype(jnp.float32).reshape(fetched.shape[0], pair_count, 2, pair_width)
        toward_first = jnp.einsum("pij,npj->npi", blocks, pair_view[:, :, 1], precision=hp)
        toward_second = jnp.einsum("pij,npi->npj", blocks, pair_view[:, :, 0], precision=hp)
        results = jnp.stack([toward_first, toward_second], axis=2).reshape(
            fetched.shape[0], end_count, pair_width
        )
        onehot = (
            jnp.arange(kpoint_local * lax.axis_size("pb"), dtype=jnp.int32)[:, None]
            == destination[None, :]
        ).astype(jnp.float32)
        screened_term = lax.psum_scatter(
            jnp.einsum("re,nej->rnj", onehot, results, precision=hp),
            "pb",
            scatter_dimension=0,
            tiled=True,
        ).transpose(1, 0, 2)
        partial_density = jnp.einsum(
            "nkj,kjm->nm", current, products, preferred_element_type=jnp.float32
        )
        density = lax.psum(partial_density, "pb").astype(jnp.bfloat16)
        potential = jnp.einsum(
            "nv,mv->nm", density, bare, preferred_element_type=jnp.float32
        ).astype(jnp.bfloat16)
        bare_term = jnp.einsum(
            "kjm,nm->nkj", products, potential, preferred_element_type=jnp.float32
        )
        return transition[None] * current.astype(jnp.float32) + 2.0 * bare_term - screened_term

    first_step = apply_kernel(trial.astype(jnp.bfloat16))
    second_step = 2.0 * apply_kernel(first_step.astype(jnp.bfloat16)) - trial
    return cheb[0] * trial + cheb[1] * first_step + cheb[2] * second_step


def solution(mesh):
    in_specs = (
        P("pb", None, "vert"),
        P("pb", None),
        P("vert", "pb", None),
        P("pb", None, "vert"),
        P(),
        P(),
        P("pb"),
        P("pb"),
        P(),
    )
    out_specs = P("vert", "pb", None)
    return jax.shard_map(body, mesh=mesh, in_specs=in_specs, out_specs=out_specs, check_vma=False)
```

profile of v0, /device:TPU:0, one launch (start us, length us, event | category | flops | bytes accessed | tf_op | source)
XLA Modules:
  0.0 234.5 jit_solution(17398259093618122066)
XLA Ops:
  6.5 0.8 fusion.40
  7.4 0.7 pad_add_fusion
  8.2 32.7 %all_gather.17 = bf16[16,32,256]{2,1,0:T(8,128)(2,1)S(1)} all-gather(bf16[2,32,256]{2,1,0:T(8,128)(2,1)} %param.11), channel_id=1, replica_groups=mesh['pb'=8,'vert'=4] {'pb'}, dimensions={0}, use_global_device_ids=true | all-gather | bytes 294912 | tf_op jit(solution)/shard_map/all_gather | solution.py:28
  41.1 0.8 select_reduce_fusion
  42.2 5.6 %all_gather.18 = bf16[6,16,1024]{2,1,0:T(8,128)(2,1)S(1)} all-gather(bf16[6,16,256]{2,1,0:T(8,128)(2,1)S(1)} %get-tuple-element.68), channel_id=1, replica_groups=mesh['pb'=8,'vert'=4] {'vert'}, dimensions={2}, use_global_device_ids=true | all-gather | bytes 245760 | tf_op jit(solution)/shard_map/all_gather | solution.py:35
  47.8 35.6 %while.10 = (s32[]{:T(128)}, f32[3,256,256]{2,1,0:T(8,128)S(1)}, s32[3]{0:T(128)S(1)}, bf16[3,2,16,1024]{3,2,1,0:T(8,128)(2,1)S(1)}, s32[3]{0:T(128)}, /*index=5...) while((s32[]{:T(128)}, f32[3,256,256]{2,1,0:T(8,128)S(1)}, ...), condition=%wide.region_3.4_spmd, body=%wide.region_2.3_spmd.sunk | while | flops 168534016 | bytes 3883225 | solution.py:66
  47.9 0.7 dynamic_slice.30
  50.6 1.3 dynamic_slice.31
  54.0 1.3 convolution_convert_fusion.7
  55.4 1.8 convolution_bitcast_fusion.8
  57.2 2.4 %broadcast_in_dim.50 = f32[1,256,256]{2,1,0:T(8,128)S(1)} reshape(f32[16,16,16,16]{3,2,1,0:T(8,128)} %convolution_bitcast_fusion.8) | data formatting | bytes 524288 | tf_op jit(solution)/shard_map/while/body/jit(dynamic_update_index_in_dim)/broadcast_in_dim | solution.py:66
  59.7 0.7 dynamic_slice.30
  62.4 1.3 dynamic_slice.31
  65.9 1.3 convolution_convert_fusion.7
  67.3 1.8 convolution_bitcast_fusion.8
  69.1 2.4 %broadcast_in_dim.50 = f32[1,256,256]{2,1,0:T(8,128)S(1)} reshape(f32[16,16,16,16]{3,2,1,0:T(8,128)} %convolution_bitcast_fusion.8) | data formatting | bytes 524288 | tf_op jit(solution)/shard_map/while/body/jit(dynamic_update_index_in_dim)/broadcast_in_dim | solution.py:66
  74.3 1.3 dynamic_slice.31
  77.8 1.3 convolution_convert_fusion.7
  79.2 1.8 convolution_bitcast_fusion.8
  81.0 2.4 %broadcast_in_dim.50 = f32[1,256,256]{2,1,0:T(8,128)S(1)} reshape(f32[16,16,16,16]{3,2,1,0:T(8,128)} %convolution_bitcast_fusion.8) | data formatting | bytes 524288 | tf_op jit(solution)/shard_map/while/body/jit(dynamic_update_index_in_dim)/broadcast_in_dim | solution.py:66
  83.5 0.9 copy-done.2
  84.4 5.4 %all_gather.15 = bf16[2,32,1024]{2,1,0:T(8,128)(2,1)S(1)} all-gather(bf16[2,32,256]{2,1,0:T(8,128)(2,1)S(1)} %copy-done.3), channel_id=1, replica_groups=mesh['pb'=8,'vert'=4] {'vert'}, dimensions={2}, use_global_device_ids=true | all-gather | bytes 163840 | tf_op jit(solution)/shard_map/all_gather | solution.py:68
  89.8 26.0 %all_gather.16 = bf16[2,16,256]{2,0,1:T(2,128)(2,1)S(1)} all-gather(bf16[2,2,256]{2,0,1:T(2,128)(2,1)S(1)} %copy.98), channel_id=1, replica_groups=mesh['pb'=8,'vert'=4] {'pb'}, dimensions={1}, use_global_device_ids=true | all-gather | bytes 18432 | tf_op jit(solution)/shard_map/all_gather | solution.py:83
  118.4 1.8 all-reduce.6.cloned.1.call-done
  120.2 1.5 convolution_bitcast_fusion.5
  121.7 1.6 convolution_bitcast_fusion.6
  123.6 37.5 %all-reduce.3 = (f32[16,2,256]{2,1,0:T(2,128)S(1)}, bf16[2,1024]{1,0:T(2,128)(2,1)S(1)}) all-reduce(f32[16,2,256]{2,1,0:T(2,128)S(1)} %copy.70, f32[2,1024]{1,0:T(2,128)S(1)} %convolution_bitcast_fusion.2), channel_id=2, replica_groups=mesh['pb'=8,'vert'=4] {'pb'}, use_global_device_ids=true, to_apply=%region_5.6.clone | all-reduce | flops 10240 | bytes 77824
  161.1 0.9 fusion.45
  162.3 26.0 %all_gather.19 = bf16[2,16,256]{2,0,1:T(2,128)(2,1)S(1)} all-gather(bf16[2,2,256]{2,0,1:T(2,128)(2,1)S(1)} %get-tuple-element.72), channel_id=1, replica_groups=mesh['pb'=8,'vert'=4] {'pb'}, dimensions={1}, use_global_device_ids=true | all-gather | bytes 18432 | tf_op jit(solution)/shard_map/all_gather | solution.py:83
  188.5 1.6 convolution_bitcast_fusion.4
  190.9 33.4 %all-reduce.2 = (f32[16,2,256]{2,1,0:T(2,128)S(1)}, bf16[2,1024]{1,0:T(2,128)(2,1)S(1)}) all-reduce(f32[16,2,256]{2,1,0:T(2,128)S(1)} %copy.77, f32[2,1024]{1,0:T(2,128)S(1)} %convolution_bitcast_fusion.1), channel_id=3, replica_groups=mesh['pb'=8,'vert'=4] {'pb'}, use_global_device_ids=true, to_apply=%region_7.8.clone | all-reduce | flops 10240 | bytes 77824
  224.2 2.8 %fusion.16 = f32[2,2,256]{2,0,1:T(2,128)S(1)} fusion(bf16[2,256,1024]{2,1,0:T(8,128)(2,1)S(1)} %bitcast.161, bf16[1024,1024]{1,0:T(8,128)(2,1)S(1)} %copy-done, f32[16,2,256]{2,1,0:T(2,128)S(1)} %get-tuple-element.57, u32[]{:T(128)S(6)} %multiply.1, bf16[2,1024]{1,0:T(2,128)(2,1)S(1)} %get-tuple-element.58, bf16[2,2,256]{2,0,1:T(2,128)(2,1)S(1)} %get-tuple-element.72, ...), kind=kOutput, calls=%fused_computation.39 | convolution fusion | flops 6305792 | bytes 3170320 | tf_op jit(solution)/shard_map/kjm,nm->nkj/dot_general | solution.py:107
  (65 shorter events, 5.7 us)
Async XLA Ops:
  6.5 154.6 %copy-start = (bf16[1024,1024]{1,0:T(8,128)(2,1)S(1)}, bf16[1024,1024]{1,0:T(8,128)(2,1)}, u32[]{:S(2)}) copy-start(bf16[1024,1024]{1,0:T(8,128)(2,1)} %param.15) | copy-start | bytes 6291460
  6.5 113.6 %all-reduce.6.cloned.1.call-start = ((), (), s32[]{:S(2)}) async-start(), calls=%async_computation | async-start | bytes 1572864 | tf_op jit(solution)/shard_map/psum | solution.py:67
  47.8 36.5 %copy-start.3 = (bf16[2,32,256]{2,1,0:T(8,128)(2,1)S(1)}, bf16[2,32,256]{2,1,0:T(8,128)(2,1)}, u32[]{:S(2)}) copy-start(bf16[2,32,256]{2,1,0:T(8,128)(2,1)} %param.11) | copy-start | bytes 98308
  47.8 42.0 %copy-start.4 = (f32[2,2,256]{2,1,0:T(2,128)S(1)}, f32[2,2,256]{2,1,0:T(2,128)}, u32[]{:S(2)}) copy-start(f32[2,2,256]{2,1,0:T(2,128)} %param.13) | copy-start | bytes 12292
  47.8 68.2 %copy-start.6 = (f32[3]{0:T(128)S(1)}, f32[3]{0:T(128)}, u32[]{:S(2)}) copy-start(f32[3]{0:T(128)} %param.16) | copy-start | bytes 40
  47.8 68.8 %copy-start.7 = (u32[32]{0:T(128)S(1)}, u32[32]{0:T(128)}, u32[]{:S(2)}) copy-start(u32[32]{0:T(128)} %constant.48) | copy-start | bytes 388
  83.4 0.9 copy-start.2
  117.9 43.2 %copy-start.5 = (f32[2,256]{1,0:T(2,128)S(1)}, f32[2,256]{1,0:T(2,128)}, u32[]{:S(2)}) copy-start(f32[2,256]{1,0:T(2,128)} %param.12) | copy-start | bytes 6148
  162.1 28.1 %copy-start.1 = (f32[3,256,256]{2,1,0:T(8,128)S(1)}, f32[3,256,256]{2,1,0:T(8,128)}, u32[]{:S(2)}) copy-start(f32[3,256,256]{2,1,0:T(8,128)} %all-reduce.6.cloned.1.call-done) | copy-start | bytes 2359300
Sparse Core Ops, SparseCore 0:
  84.5 35.6 all-reduce.5
where the time goes:
time: 235 us
  blocking collectives  167 us (71%)
  matrix products  19.9 us (8%)
  local copies, waits for them, and re-layouts  16.5 us (7%)
  between operations  14.2 us (6%)
  loops' own time  12.5 us (5%)
  other arithmetic  2.88 us (1%)
    unnamed x2, blocking collectives  70.9 us
    all_gather x2, blocking collectives, apply_kernel(): lax.all_gather(current, 'pb', axis=1, tiled=True)  52 us
    all_gather x1, blocking collectives, body(): shard_piece = lax.all_gather(orbitals, 'pb', axis=0, tiled=True)  32.7 us
    another operation x1, loops' own time, body(): block_parts = lax.map(build_block, jnp.arange(pair_count, dtype=jnp.int32))  12.5 us
    broadcast_in_dim x3, local copies, waits for them, and re-layouts, body(): block_parts = lax.map(build_block, jnp.arange(pair_count, dtype=jnp.int32))  7.32 us
    all_gather x1, blocking collectives, body(): lax.all_gather(picked[:, :valence, :], 'vert', axis=2, tiled=True)  5.61 us
    all_gather x1, blocking collectives, body(): lax.all_gather(orbitals, 'vert', axis=2, tiled=True).astype(jnp.float32)  5.43 us
    dot_general x3, matrix products, build_block(): lax.dot_general(half_product, right_pair, (((1,), (1,)), ((), ())), prefe...  5.37 us
  transfers between devices with their start and end apart: 1, of which 1 were waited for; matrix products, arithmetic and copies ran while one was open for 1% of the time, Pallas kernels for 0%

commit v1 on v0

v1 whole, which is shorter than its diff:
```python
import functools

import jax
import jax.numpy as jnp
from jax import lax
from jax.experimental import pallas as pl
from jax.experimental.pallas import tpu as pltpu
from jax.sharding import PartitionSpec as P

NV = 16
LANES = 128
MESH = pl.DeviceIdType.MESH
F32 = jnp.float32
BF16 = jnp.bfloat16
TRANSPOSED = (((1,), (1,)), ((), ()))


def kernel(
    pn, vn, orb, trans, trial, scr, bare, cheb, pair_k, pair_slot, k_order, out,
    orb_all, x_all, x_own, x_tile, trial_tile, trans_tile, proj, val_own, val_all, half,
    dens_own, dens_all, bare_own, weighted, result, bare_part, part, part_all,
    bare_sem, orb_sem, val_sem, x_sem, dens_sem, part_sem,
):
    me_p, me_v = lax.axis_index("pb"), lax.axis_index("vert")
    count = pn * vn
    me = me_p * vn + me_v
    kl, bands, ml = orb.shape
    valence = NV
    cond = bands - valence
    width = valence * cond
    nl = trial.shape[0]
    nvec = nl * vn
    pairs = pair_k.shape[0]
    ktot = k_order.shape[0]
    rows = valence * nvec
    halves = width // LANES

    barrier = pltpu.get_barrier_semaphore()

    @pl.loop(1, count)
    def _(i):
        t = lax.rem(me + i, count)
        pl.semaphore_signal(barrier, inc=1, device_id=(t // vn, lax.rem(t, vn)), device_id_type=MESH)

    bare_copy = pltpu.make_async_copy(bare.at[pl.ds(pl.multiple_of(me_v * ml, ml), ml)], bare_own, bare_sem)
    bare_copy.start()
    for h in range(halves):
        for k in range(kl):
            for n in range(nl):
                at = (h * kl + k) * nl + n
                cols = slice(h * LANES, (h + 1) * LANES)
                trial_tile[at : at + 1, :] = trial[n, k : k + 1, cols]
                trans_tile[at : at + 1, :] = trans[k : k + 1, cols]
    x_own[0] = trial_tile[...]
    orb_all[pl.ds(me_p * kl, kl)] = orb[...]

    ends = []
    for p in range(pairs):
        first = pair_k[p]
        second = lax.rem(first - (me_p * kl + pair_slot[p]) + ktot, ktot)
        ends += [first, second]

    def find(r, found):
        key = k_order[r]
        return tuple(jnp.where(key == e, r, f) for e, f in zip(ends, found))

    dest = lax.fori_loop(0, ktot, find, tuple(jnp.int32(0) for _ in ends))

    pl.semaphore_wait(barrier, count - 1)

    def orb_send(i):
        return pltpu.make_async_remote_copy(
            src_ref=orb, dst_ref=orb_all.at[pl.ds(me_p * kl, kl)], send_sem=orb_sem.at[0],
            recv_sem=orb_sem.at[1], device_id=(lax.rem(me_p + i, pn), me_v), device_id_type=MESH)

    @pl.loop(1, pn)
    def _(i):
        orb_send(i).start()

    def x_send(a):
        x_all[a, me] = x_own[a]

        @pl.loop(1, count)
        def _(i):
            t = lax.rem(me + i, count)
            pltpu.make_async_remote_copy(
                src_ref=x_own.at[a], dst_ref=x_all.at[a, me], send_sem=x_sem.at[0, a],
                recv_sem=x_sem.at[1, a], device_id=(t // vn, lax.rem(t, vn)), device_id_type=MESH).start()

    def vert_send(src, dst, sems):
        @pl.loop(1, vn)
        def _(i):
            pltpu.make_async_remote_copy(
                src_ref=src, dst_ref=dst.at[me_v], send_sem=sems[0], recv_sem=sems[1],
                device_id=(me_p, lax.rem(me_v + i, vn)), device_id_type=MESH).start()

    def drain(ref, sem):
        pltpu.make_async_copy(ref, ref, sem).wait()

    x_send(0)
    drain(orb_all.at[pl.ds(0, (pn - 1) * kl)], orb_sem.at[1])
    for e in range(2 * pairs):
        val_own[e] = orb_all[dest[e], 0:valence, :]
    val_all[me_v] = val_own[...]
    vert_send(val_own, val_all, (val_sem.at[0], val_sem.at[1]))

    own_block = (
        lax.broadcasted_iota(jnp.int32, (rows, width), 0) // nvec
        == lax.broadcasted_iota(jnp.int32, (rows, width), 1) // cond
    )

    def tiled(r):
        return jnp.concatenate([orb_all[r, valence:bands, :]] * valence, axis=0)

    def back(value, r):
        spread = lax.dot_general(value.astype(BF16), tiled(r), TRANSPOSED, preferred_element_type=F32)
        spread = jnp.where(own_block, spread, 0.0)
        return jnp.sum(spread.reshape(valence, nvec, width), axis=0)

    def apply_kernel(a):
        drain(x_all.at[a, pl.ds(0, count - 1)], x_sem.at[1, a])

        def project(d, density):
            for k in range(kl):
                r = d * kl + k
                for w in range(vn):
                    for h in range(halves):
                        at = (h * kl + k) * nl
                        x_tile[w * nl : (w + 1) * nl, h * LANES : (h + 1) * LANES] = x_all[
                            a, d * vn + w, at : at + nl, :]
                wide = jnp.where(own_block, jnp.concatenate([x_tile[...]] * valence, axis=0), 0.0)
                y = jnp.dot(wide.astype(BF16), tiled(r), preferred_element_type=F32)
                proj[r] = y
                vals = orb_all[r, 0:valence, :].astype(F32)
                for v in range(valence):
                    density = density + y[v * nvec : (v + 1) * nvec] * vals[v : v + 1]
            return density

        density = lax.fori_loop(0, pn, project, jnp.zeros((nvec, ml), F32))
        dens_own[a] = density
        dens_all[a, me_v] = density
        vert_send(dens_own.at[a], dens_all.at[a], (dens_sem.at[0, a], dens_sem.at[1, a]))

        if a == 0:
            drain(val_all.at[pl.ds(0, vn - 1)], val_sem.at[1])
            for p in range(pairs):
                def add(w, total, p=p):
                    one = val_all[w, 2 * p].astype(F32)
                    two = val_all[w, 2 * p + 1].astype(F32)
                    left = jnp.concatenate(
                        [(one[v : v + 1] * two).astype(BF16) for v in range(valence)], axis=0)
                    matrix = scr[pair_slot[p], pl.ds(pl.multiple_of(w * ml, ml), ml), :]
                    return total + jnp.dot(left, matrix, preferred_element_type=F32)

                total = lax.fori_loop(0, vn, add, jnp.zeros((valence * valence, ml), F32))
                half[p] = total.astype(BF16).astype(F32).reshape(valence, valence, ml)

        for p in range(pairs):
            @pl.loop(0, valence)
            def _(v, p=p):
                total = jnp.zeros((nvec, ml), F32)
                other = jnp.zeros((nvec, ml), F32)
                line = half[p, v]
                for u in range(valence):
                    total = total + line[u : u + 1] * proj[dest[2 * p + 1], u * nvec : (u + 1) * nvec, :]
                    other = other + half[p, u, pl.ds(v, 1), :] * proj[dest[2 * p], u * nvec : (u + 1) * nvec, :]
                here = pl.ds(pl.multiple_of(v * nvec, nvec), nvec)
                weighted[0, here] = total
                weighted[1, here] = other

            result[2 * p] = back(weighted[0], dest[2 * p])
            result[2 * p + 1] = back(weighted[1], dest[2 * p + 1])

        drain(dens_all.at[a, pl.ds(0, vn - 1)], dens_sem.at[1, a])
        if a == 0:
            bare_copy.wait()
        potential = jnp.zeros((nvec, ml), F32)
        for w in range(vn):
            potential = potential + lax.dot_general(
                dens_all[a, w].astype(BF16), bare_own[:, w * ml : (w + 1) * ml], TRANSPOSED,
                preferred_element_type=F32)
        potential = potential.astype(BF16).astype(F32)
        for k in range(kl):
            vals = orb[k, 0:valence, :].astype(F32)
            value = jnp.concatenate([vals[v : v + 1] * potential for v in range(valence)], axis=0)
            bare_part[k] = 2.0 * back(value, me_p * kl + k)

        @pl.loop(0, pn)
        def _(d):
            mine = jnp.where(d == me_p, 1.0, 0.0)
            for k in range(kl):
                total = mine * bare_part[k]
                for e in range(2 * pairs):
                    total = total - jnp.where(dest[e] == d * kl + k, 1.0, 0.0) * result[e]
                for w in range(vn):
                    for h in range(halves):
                        at = (h * kl + k) * nl
                        part[a, d * vn + w, at : at + nl, :] = total[
                            w * nl : (w + 1) * nl, h * LANES : (h + 1) * LANES]

        part_all[a, me] = part[a, me]

        @pl.loop(1, count)
        def _(i):
            t = lax.rem(me + i, count)
            pltpu.make_async_remote_copy(
                src_ref=part.at[a, t], dst_ref=part_all.at[a, me], send_sem=part_sem.at[0, a],
                recv_sem=part_sem.at[1, a], device_id=(t // vn, lax.rem(t, vn)), device_id_type=MESH).start()

        drain(part_all.at[a, pl.ds(0, count - 1)], part_sem.at[1, a])
        total = jnp.sum(part_all[a], axis=0)
        current = x_own[a].astype(BF16).astype(F32)
        return trans_tile[...] * current + total

    first_step = apply_kernel(0)
    x_own[1] = first_step
    x_send(1)
    second_step = 2.0 * apply_kernel(1) - trial_tile[...]
    filtered = cheb[0] * trial_tile[...] + cheb[1] * x_own[1] + cheb[2] * second_step
    for h in range(halves):
        for k in range(kl):
            for n in range(nl):
                at = (h * kl + k) * nl + n
                out[n, k : k + 1, h * LANES : (h + 1) * LANES] = filtered[at : at + 1]

    drain(orb_all.at[pl.ds(0, (pn - 1) * kl)], orb_sem.at[0])
    drain(val_all.at[pl.ds(0, vn - 1)], val_sem.at[0])
    for a in range(2):
        drain(x_all.at[a, pl.ds(0, count - 1)], x_sem.at[0, a])
        drain(dens_all.at[a, pl.ds(0, vn - 1)], dens_sem.at[0, a])
        drain(part_all.at[a, pl.ds(0, count - 1)], part_sem.at[0, a])


def body(pn, vn, orbitals, transition, trial, screened, bare, cheb, pair_k, pair_slot, k_order):
    kl, bands, ml = orbitals.shape
    nl, _, width = trial.shape
    pairs = pair_k.shape[0]
    ktot = k_order.shape[0]
    nvec = nl * vn
    count = pn * vn
    tile = (nl * kl * width // LANES, LANES)
    vmem = pl.BlockSpec(memory_space=pltpu.VMEM)
    smem = pl.BlockSpec(memory_space=pltpu.SMEM)
    dma = pltpu.SemaphoreType.DMA
    return pl.pallas_call(
        functools.partial(kernel, pn, vn),
        out_shape=jax.ShapeDtypeStruct(trial.shape, F32),
        in_specs=[vmem, vmem, vmem, vmem, pl.BlockSpec(memory_space=pl.ANY), smem, smem, smem, smem],
        out_specs=vmem,
        scratch_shapes=[
            pltpu.VMEM((ktot, bands, ml), BF16),
            pltpu.VMEM((2, count) + tile, F32),
            pltpu.VMEM((2,) + tile, F32),
            pltpu.VMEM((nvec, width), F32),
            pltpu.VMEM(tile, F32),
            pltpu.VMEM(tile, F32),
            pltpu.VMEM((ktot, NV * nvec, ml), F32),
            pltpu.VMEM((2 * pairs, NV, ml), BF16),
            pltpu.VMEM((vn, 2 * pairs, NV, ml), BF16),
            pltpu.VMEM((pairs, NV, NV, ml), F32),
            pltpu.VMEM((2, nvec, ml), F32),
            pltpu.VMEM((2, vn, nvec, ml), F32),
            pltpu.VMEM((ml, vn * ml), BF16),
            pltpu.VMEM((2, NV * nvec, ml), F32),
            pltpu.VMEM((2 * pairs, nvec, width), F32),
            pltpu.VMEM((kl, nvec, width), F32),
            pltpu.VMEM((2, count) + tile, F32),
            pltpu.VMEM((2, count) + tile, F32),
            dma, dma((2,)), dma((2,)), dma((2, 2)), dma((2, 2)), dma((2, 2)),
        ],
        compiler_params=pltpu.CompilerParams(
            collective_id=0, has_side_effects=True, vmem_limit_bytes=56 * 2**20),
    )(orbitals, transition, trial, screened, bare, cheb, pair_k, pair_slot, k_order)


def solution(mesh):
    in_specs = (
        P("pb", None, "vert"),
        P("pb", None),
        P("vert", "pb", None),
        P("pb", None, "vert"),
        P(),
        P(),
        P("pb"),
        P("pb"),
        P(),
    )
    out_specs = P("vert", "pb", None)
    step = functools.partial(body, mesh.shape["pb"], mesh.shape["vert"])
    return jax.shard_map(step, mesh=mesh, in_specs=in_specs, out_specs=out_specs, check_vma=False)
```

time: 235 us -> 50 us (0.21)
  blocking collectives: 167 us -> 0 us
  Pallas kernels: 0 us -> 48.5 us
  matrix products: 19.9 us -> 0 us
  local copies, waits for them, and re-layouts: 16.5 us -> 1.28 us
  between operations: 14.2 us -> 0.01 us
  loops' own time: 12.5 us -> 0 us
  other arithmetic: 2.88 us -> 0 us
    all_gather x5 -> x0, blocking collectives: 95.7 us -> none  [the longest x2 52 us: apply_kernel(): lax.all_gather(current, 'pb', axis=1, tiled=True)]
    unnamed x2 -> x0, blocking collectives: 70.9 us -> none
    pallas_call x0 -> x1, Pallas kernels: none -> 48.5 us  [body(): pl.pallas_call(functools.partial(kernel, pn, vn), out_shape=jax.ShapeDtyp...]
    dot_general x19 -> x0, matrix products: 19.9 us -> none  [the longest x3 5.37 us: build_block(): lax.dot_general(half_product, right_pair, (((1,), (1,)), ((), ())), prefe...]
    another operation x1 -> x0, loops' own time: 12.5 us -> none  [body(): block_parts = lax.map(build_block, jnp.arange(pair_count, dtype=jnp.int32))]
    broadcast_in_dim x3 -> x0, local copies, waits for them, and re-layouts: 7.32 us -> none  [body(): block_parts = lax.map(build_block, jnp.arange(pair_count, dtype=jnp.int32))]
    dynamic_slice x6 -> x0, local copies, waits for them, and re-layouts: 5.9 us -> none  [the longest x3 3.93 us: build_block(): matrix = screened[pair_slot[pair_index]]]
  transfers between devices with their start and end apart: 1 -> 0, of which waited for: 1 -> 0; matrix products, arithmetic and copies ran while one was open for 1% -> 0% of each run, Pallas kernels for 0% -> 0%
where the time goes in v1:
time: 50 us; the launch traced here: 49.8 us
  Pallas kernels  48.5 us (97%)
  local copies, waits for them, and re-layouts  1.28 us (3%)
    pallas_call x1, Pallas kernels, body(): pl.pallas_call(functools.partial(kernel, pn, vn), out_shape=jax.ShapeDtyp...  48.5 us
    unnamed x1, local copies, waits for them, and re-layouts  1.28 us

profile of v1, /device:TPU:0, one launch (start us, length us, event | category | flops | bytes accessed | tf_op | source)
XLA Modules:
  0.0 49.8 jit_solution(5256018187098828199)
XLA Ops:
  0.0 48.5 %shard_map.91 = f32[2,2,256]{2,1,0:T(2,128)} custom-call(bf16[2,32,256]{2,1,0:T(8,128)(2,1)} %orb.1, f32[2,256]{1,0:T(2,128)} %trans.1, f32[2,2,256]{2,1,0:T(2,128)} %trial.1, bf16[2,1024,256]{2,1,0:T(8,128)(2,1)} %scr.1, bf16[1024,1024]{1,0:T(8,128)(2,1)} %bare.1, f32[3]{0:T(128)} %cheb.1, s32[3]{0:T(128)} %pair_k.1, s32[3]{0:T(128)} %pair_slot.1, s32[16]{0:T(128)} %k_order.1), custom_call_target="tpu_custom_call" | custom-call | tf_op jit(solution)/shard_map/pallas_call | solution.py:245
  48.5 1.3 %copy.11 = f32[2,2,256]{2,1,0:T(2,128)} copy(f32[2,2,256]{2,1,0:T(2,128)} %shard_map.91) | data formatting | bytes 8192

commit v2 on v1

--- a/solution.py
+++ b/solution.py
@@ -17,9 +17,9 @@
 
 def kernel(
     pn, vn, orb, trans, trial, scr, bare, cheb, pair_k, pair_slot, k_order, out,
-    orb_all, x_all, x_own, x_tile, trial_tile, trans_tile, proj, val_own, val_all, half,
+    orb_all, x_all, x_own, x_tile, trial_tile, trans_tile, proj, val_own, val_all, left, half,
     dens_own, dens_all, bare_own, weighted, result, bare_part, part, part_all,
-    bare_sem, orb_sem, val_sem, x_sem, dens_sem, part_sem,
+    bare_sem, orb_sem, orb_recv, val_sem, x_sem, dens_sem, part_sem,
 ):
     me_p, me_v = lax.axis_index("pb"), lax.axis_index("vert")
     count = pn * vn
@@ -68,14 +68,25 @@
 
     pl.semaphore_wait(barrier, count - 1)
 
-    def orb_send(i):
-        return pltpu.make_async_remote_copy(
-            src_ref=orb, dst_ref=orb_all.at[pl.ds(me_p * kl, kl)], send_sem=orb_sem.at[0],
-            recv_sem=orb_sem.at[1], device_id=(lax.rem(me_p + i, pn), me_v), device_id_type=MESH)
-
-    @pl.loop(1, pn)
+    def drain(ref, sem):
+        pltpu.make_async_copy(ref, ref, sem).wait()
+
+    partner = me_p + 1 - 2 * lax.rem(me_p, 2)
+
+    def orb_send(block, src, to):
+        pltpu.make_async_remote_copy(
+            src_ref=src, dst_ref=orb_all.at[pl.ds(block * kl, kl)], send_sem=orb_sem,
+            recv_sem=orb_recv.at[block], device_id=(to, me_v), device_id_type=MESH).start()
+
+    def orb_wait(block):
+        here = orb_all.at[pl.ds(block * kl, kl)]
+        drain(here, orb_recv.at[block])
+
+    @pl.loop(1, pn // 2)
     def _(i):
-        orb_send(i).start()
+        orb_send(me_p, orb, lax.rem(me_p + 2 * i, pn))
+
+    orb_send(me_p, orb, partner)
 
     def x_send(a):
         x_all[a, me] = x_own[a]
@@ -94,15 +105,13 @@
                 src_ref=src, dst_ref=dst.at[me_v], send_sem=sems[0], recv_sem=sems[1],
                 device_id=(me_p, lax.rem(me_v + i, vn)), device_id_type=MESH).start()
 
-    def drain(ref, sem):
-        pltpu.make_async_copy(ref, ref, sem).wait()
-
     x_send(0)
-    drain(orb_all.at[pl.ds(0, (pn - 1) * kl)], orb_sem.at[1])
-    for e in range(2 * pairs):
-        val_own[e] = orb_all[dest[e], 0:valence, :]
-    val_all[me_v] = val_own[...]
-    vert_send(val_own, val_all, (val_sem.at[0], val_sem.at[1]))
+
+    @pl.loop(1, pn // 2)
+    def _(i):
+        block = lax.rem(me_p + pn - 2 * i, pn)
+        orb_wait(block)
+        orb_send(block, orb_all.at[pl.ds(block * kl, kl)], partner)
 
     own_block = (
         lax.broadcasted_iota(jnp.int32, (rows, width), 0) // nvec
@@ -136,7 +145,19 @@
                     density = density + y[v * nvec : (v + 1) * nvec] * vals[v : v + 1]
             return density
 
-        density = lax.fori_loop(0, pn, project, jnp.zeros((nvec, ml), F32))
+        density = lax.fori_loop(
+            0, pn // 2, lambda i, t: project(lax.rem(me_p + pn - 2 * i, pn), t), jnp.zeros((nvec, ml), F32))
+        if a == 0:
+            @pl.loop(0, pn // 2)
+            def _(i):
+                orb_wait(lax.rem(partner + pn - 2 * i, pn))
+
+            for e in range(2 * pairs):
+                val_own[e] = orb_all[dest[e], 0:valence, :]
+            val_all[me_v] = val_own[...]
+            vert_send(val_own, val_all, (val_sem.at[0], val_sem.at[1]))
+        density = lax.fori_loop(
+            0, pn // 2, lambda i, t: project(lax.rem(partner + pn - 2 * i, pn), t), density)
         dens_own[a] = density
         dens_all[a, me_v] = density
         vert_send(dens_own.at[a], dens_all.at[a], (dens_sem.at[0, a], dens_sem.at[1, a]))
@@ -144,32 +165,66 @@
         if a == 0:
             drain(val_all.at[pl.ds(0, vn - 1)], val_sem.at[1])
             for p in range(pairs):
-                def add(w, total, p=p):
+                for w in range(vn):
                     one = val_all[w, 2 * p].astype(F32)
                     two = val_all[w, 2 * p + 1].astype(F32)
-                    left = jnp.concatenate(
-                        [(one[v : v + 1] * two).astype(BF16) for v in range(valence)], axis=0)
-                    matrix = scr[pair_slot[p], pl.ds(pl.multiple_of(w * ml, ml), ml), :]
-                    return total + jnp.dot(left, matrix, preferred_element_type=F32)
-
-                total = lax.fori_loop(0, vn, add, jnp.zeros((valence * valence, ml), F32))
+                    for v in range(valence):
+                        left[p, v * valence : (v + 1) * valence, w * ml : (w + 1) * ml] = (
+                            one[v : v + 1] * two).astype(BF16)
+                total = jnp.dot(left[p], scr[pair_slot[p]], preferred_element_type=F32)
                 half[p] = total.astype(BF16).astype(F32).reshape(valence, valence, ml)
 
         for p in range(pairs):
-            @pl.loop(0, valence)
-            def _(v, p=p):
-                total = jnp.zeros((nvec, ml), F32)
-                other = jnp.zeros((nvec, ml), F32)
-                line = half[p, v]
+            for h in range(ml // LANES):
+                cols = slice(h * LANES, (h + 1) * LANES)
+                ahead = [proj[dest[2 * p + 1], u * nvec : (u + 1) * nvec, cols] for u in range(valence)]
+
+                def contract(v, other, p=p, cols=cols, ahead=ahead):
+                    here = pl.ds(pl.multiple_of(v * nvec, nvec), nvec)
+                    line = half[p, v, :, cols]
+                    mine = proj[dest[2 * p], here, cols]
+                    sums, kept = [], []
+                    for u in range(valence):
+                        spread = jnp.broadcast_to(line[u : u + 1], (nvec, LANES))
+                        sums.append(spread * ahead[u])
+                        kept.append(other[u] + spread * mine)
+                    while len(sums) > 1:
+                        sums = [sum(sums[i : i + 2]) for i in range(0, len(sums), 2)]
+                    weighted[2 * p, here, cols] = sums[0]
+                    return tuple(kept)
+
+                zero = jnp.zeros((nvec, LANES), F32)
+                other = lax.fori_loop(0, valence, contract, (zero,) * valence)
                 for u in range(valence):
-                    total = total + line[u : u + 1] * proj[dest[2 * p + 1], u * nvec : (u + 1) * nvec, :]
-                    other = other + half[p, u, pl.ds(v, 1), :] * proj[dest[2 * p], u * nvec : (u + 1) * nvec, :]
-                here = pl.ds(pl.multiple_of(v * nvec, nvec), nvec)
-                weighted[0, here] = total
-                weighted[1, here] = other
-
-            result[2 * p] = back(weighted[0], dest[2 * p])
-            result[2 * p + 1] = back(weighted[1], dest[2 * p + 1])
+                    weighted[2 * p + 1, u * nvec : (u + 1) * nvec, cols] = other[u]
+
+        for e in range(2 * pairs):
+            result[e] = back(weighted[e], dest[e])
+
+        def assemble(d, own):
+            for k in range(kl):
+                total = bare_part[k] if own else jnp.zeros((nvec, width), F32)
+                for e in range(2 * pairs):
+                    total = total - jnp.where(dest[e] == d * kl + k, 1.0, 0.0) * result[e]
+                for w in range(vn):
+                    for h in range(halves):
+                        at = (h * kl + k) * nl
+                        part[a, d * vn + w, at : at + nl, :] = total[
+                            w * nl : (w + 1) * nl, h * LANES : (h + 1) * LANES]
+
+        def part_send(d, w):
+            pltpu.make_async_remote_copy(
+                src_ref=part.at[a, d * vn + w], dst_ref=part_all.at[a, me], send_sem=part_sem.at[0, a],
+                recv_sem=part_sem.at[1, a], device_id=(d, w), device_id_type=MESH).start()
+
+        @pl.loop(1, pn)
+        def _(i):
+            d = lax.rem(me_p + i, pn)
+            assemble(d, False)
+
+            @pl.loop(0, vn)
+            def _(w):
+                part_send(d, lax.rem(me_v + w, vn))
 
         drain(dens_all.at[a, pl.ds(0, vn - 1)], dens_sem.at[1, a])
         if a == 0:
@@ -184,29 +239,13 @@
             vals = orb[k, 0:valence, :].astype(F32)
             value = jnp.concatenate([vals[v : v + 1] * potential for v in range(valence)], axis=0)
             bare_part[k] = 2.0 * back(value, me_p * kl + k)
-
-        @pl.loop(0, pn)
-        def _(d):
-            mine = jnp.where(d == me_p, 1.0, 0.0)
-            for k in range(kl):
-                total = mine * bare_part[k]
-                for e in range(2 * pairs):
-                    total = total - jnp.where(dest[e] == d * kl + k, 1.0, 0.0) * result[e]
-                for w in range(vn):
-                    for h in range(halves):
-                        at = (h * kl + k) * nl
-                        part[a, d * vn + w, at : at + nl, :] = total[
-                            w * nl : (w + 1) * nl, h * LANES : (h + 1) * LANES]
+        assemble(me_p, True)
+
+        @pl.loop(1, vn)
+        def _(w):
+            part_send(me_p, lax.rem(me_v + w, vn))
 
         part_all[a, me] = part[a, me]
-
-        @pl.loop(1, count)
-        def _(i):
-            t = lax.rem(me + i, count)
-            pltpu.make_async_remote_copy(
-                src_ref=part.at[a, t], dst_ref=part_all.at[a, me], send_sem=part_sem.at[0, a],
-                recv_sem=part_sem.at[1, a], device_id=(t // vn, lax.rem(t, vn)), device_id_type=MESH).start()
-
         drain(part_all.at[a, pl.ds(0, count - 1)], part_sem.at[1, a])
         total = jnp.sum(part_all[a], axis=0)
         current = x_own[a].astype(BF16).astype(F32)
@@ -223,7 +262,7 @@
                 at = (h * kl + k) * nl + n
                 out[n, k : k + 1, h * LANES : (h + 1) * LANES] = filtered[at : at + 1]
 
-    drain(orb_all.at[pl.ds(0, (pn - 1) * kl)], orb_sem.at[0])
+    drain(orb_all.at[pl.ds(0, (pn - 1) * kl)], orb_sem)
     drain(val_all.at[pl.ds(0, vn - 1)], val_sem.at[0])
     for a in range(2):
         drain(x_all.at[a, pl.ds(0, count - 1)], x_sem.at[0, a])
@@ -257,16 +296,17 @@
             pltpu.VMEM((ktot, NV * nvec, ml), F32),
             pltpu.VMEM((2 * pairs, NV, ml), BF16),
             pltpu.VMEM((vn, 2 * pairs, NV, ml), BF16),
+            pltpu.VMEM((pairs, NV * NV, vn * ml), BF16),
             pltpu.VMEM((pairs, NV, NV, ml), F32),
             pltpu.VMEM((2, nvec, ml), F32),
             pltpu.VMEM((2, vn, nvec, ml), F32),
             pltpu.VMEM((ml, vn * ml), BF16),
-            pltpu.VMEM((2, NV * nvec, ml), F32),
+            pltpu.VMEM((2 * pairs, NV * nvec, ml), F32),
             pltpu.VMEM((2 * pairs, nvec, width), F32),
             pltpu.VMEM((kl, nvec, width), F32),
             pltpu.VMEM((2, count) + tile, F32),
             pltpu.VMEM((2, count) + tile, F32),
-            dma, dma((2,)), dma((2,)), dma((2, 2)), dma((2, 2)), dma((2, 2)),
+            dma, dma, dma((pn,)), dma((2,)), dma((2, 2)), dma((2, 2)), dma((2, 2)),
         ],
         compiler_params=pltpu.CompilerParams(
             collective_id=0, has_side_effects=True, vmem_limit_bytes=56 * 2**20),

time: 50 us -> 45.7 us (0.914)
  Pallas kernels: 48.5 us -> 44.3 us
    pallas_call x1, Pallas kernels: 48.5 us -> 44.3 us  [body(): pl.pallas_call(functools.partial(kernel, pn, vn), out_shape=jax.ShapeDtyp...]
where the time goes in v2:
time: 45.7 us; the launch traced here: 45.6 us
  Pallas kernels  44.3 us (97%)
  local copies, waits for them, and re-layouts  1.28 us (3%)
    pallas_call x1, Pallas kernels, body(): pl.pallas_call(functools.partial(kernel, pn, vn), out_shape=jax.ShapeDtyp...  44.3 us
    unnamed x1, local copies, waits for them, and re-layouts  1.28 us

profile of v2, /device:TPU:0, one launch (start us, length us, event | category | flops | bytes accessed | tf_op | source)
XLA Modules:
  0.0 45.6 jit_solution(4569127010312052352)
XLA Ops:
  0.0 44.3 %shard_map.91 = f32[2,2,256]{2,1,0:T(2,128)} custom-call(bf16[2,32,256]{2,1,0:T(8,128)(2,1)} %orb.1, f32[2,256]{1,0:T(2,128)} %trans.1, f32[2,2,256]{2,1,0:T(2,128)} %trial.1, bf16[2,1024,256]{2,1,0:T(8,128)(2,1)} %scr.1, bf16[1024,1024]{1,0:T(8,128)(2,1)} %bare.1, f32[3]{0:T(128)} %cheb.1, s32[3]{0:T(128)} %pair_k.1, s32[3]{0:T(128)} %pair_slot.1, s32[16]{0:T(128)} %k_order.1), custom_call_target="tpu_custom_call" | custom-call | tf_op jit(solution)/shard_map/pallas_call | solution.py:284
  44.3 1.3 %copy.11 = f32[2,2,256]{2,1,0:T(2,128)} copy(f32[2,2,256]{2,1,0:T(2,128)} %shard_map.91) | data formatting | bytes 8192

commit v3 on v2

--- a/solution.py
+++ b/solution.py
@@ -16,10 +16,10 @@
 
 
 def kernel(
-    pn, vn, orb, trans, trial, scr, bare, cheb, pair_k, pair_slot, k_order, out,
-    orb_all, x_all, x_own, x_tile, trial_tile, trans_tile, proj, val_own, val_all, left, half,
+    pn, vn, orb, trans, trial, scr_hbm, bare, cheb, pair_k, pair_slot, k_order, out,
+    orb_all, x_all, x_own, x_tile, trial_tile, trans_tile, proj, val_own, val_all, left, half, scr,
     dens_own, dens_all, bare_own, weighted, result, bare_part, part, part_all,
-    bare_sem, orb_sem, orb_recv, val_sem, x_sem, dens_sem, part_sem,
+    scr_sem, bare_sem, orb_sem, orb_recv, val_sem, x_sem, dens_sem, part_sem,
 ):
     me_p, me_v = lax.axis_index("pb"), lax.axis_index("vert")
     count = pn * vn
@@ -44,6 +44,8 @@
 
     bare_copy = pltpu.make_async_copy(bare.at[pl.ds(pl.multiple_of(me_v * ml, ml), ml)], bare_own, bare_sem)
     bare_copy.start()
+    scr_copy = pltpu.make_async_copy(scr_hbm, scr, scr_sem)
+    scr_copy.start()
     for h in range(halves):
         for k in range(kl):
             for n in range(nl):
@@ -129,15 +131,15 @@
     def apply_kernel(a):
         drain(x_all.at[a, pl.ds(0, count - 1)], x_sem.at[1, a])
 
-        def project(d, density):
+        def project(d, density, turn):
             for k in range(kl):
                 r = d * kl + k
                 for w in range(vn):
                     for h in range(halves):
                         at = (h * kl + k) * nl
-                        x_tile[w * nl : (w + 1) * nl, h * LANES : (h + 1) * LANES] = x_all[
+                        x_tile[turn * kl + k, w * nl : (w + 1) * nl, h * LANES : (h + 1) * LANES] = x_all[
                             a, d * vn + w, at : at + nl, :]
-                wide = jnp.where(own_block, jnp.concatenate([x_tile[...]] * valence, axis=0), 0.0)
+                wide = jnp.where(own_block, jnp.concatenate([x_tile[turn * kl + k]] * valence, axis=0), 0.0)
                 y = jnp.dot(wide.astype(BF16), tiled(r), preferred_element_type=F32)
                 proj[r] = y
                 vals = orb_all[r, 0:valence, :].astype(F32)
@@ -145,8 +147,17 @@
                     density = density + y[v * nvec : (v + 1) * nvec] * vals[v : v + 1]
             return density
 
-        density = lax.fori_loop(
-            0, pn // 2, lambda i, t: project(lax.rem(me_p + pn - 2 * i, pn), t), jnp.zeros((nvec, ml), F32))
+        def project_side(start, density):
+            turns = 2 if pn % 4 == 0 else 1
+
+            def step(i, t):
+                for turn in range(turns):
+                    t = project(lax.rem(start + pn - 2 * (turns * i + turn), pn), t, turn)
+                return t
+
+            return lax.fori_loop(0, pn // 2 // turns, step, density)
+
+        density = project_side(me_p, jnp.zeros((nvec, ml), F32))
         if a == 0:
             @pl.loop(0, pn // 2)
             def _(i):
@@ -155,24 +166,32 @@
             for e in range(2 * pairs):
                 val_own[e] = orb_all[dest[e], 0:valence, :]
             val_all[me_v] = val_own[...]
-            vert_send(val_own, val_all, (val_sem.at[0], val_sem.at[1]))
-        density = lax.fori_loop(
-            0, pn // 2, lambda i, t: project(lax.rem(partner + pn - 2 * i, pn), t), density)
+            vert_send(val_own, val_all, (val_sem.at[vn], val_sem.at[me_v]))
+        density = project_side(partner, density)
         dens_own[a] = density
         dens_all[a, me_v] = density
         vert_send(dens_own.at[a], dens_all.at[a], (dens_sem.at[0, a], dens_sem.at[1, a]))
 
         if a == 0:
-            drain(val_all.at[pl.ds(0, vn - 1)], val_sem.at[1])
-            for p in range(pairs):
-                for w in range(vn):
+            scr_copy.wait()
+            sibling = me_v + 1 - 2 * lax.rem(me_v, 2)
+            order = [lax.rem(side + 2 * j, vn) for j in range(vn // 2) for side in (me_v, sibling)]
+            for place, w in enumerate(order):
+                if place:
+                    drain(val_all.at[w], val_sem.at[w])
+                for p in range(pairs):
                     one = val_all[w, 2 * p].astype(F32)
                     two = val_all[w, 2 * p + 1].astype(F32)
                     for v in range(valence):
-                        left[p, v * valence : (v + 1) * valence, w * ml : (w + 1) * ml] = (
-                            one[v : v + 1] * two).astype(BF16)
-                total = jnp.dot(left[p], scr[pair_slot[p]], preferred_element_type=F32)
-                half[p] = total.astype(BF16).astype(F32).reshape(valence, valence, ml)
+                        left[p, v * valence : (v + 1) * valence, :] = (one[v : v + 1] * two).astype(BF16)
+                for p in range(pairs):
+                    matrix = scr[pair_slot[p], pl.ds(pl.multiple_of(w * ml, ml), ml), :]
+                    total = jnp.dot(left[p], matrix, preferred_element_type=F32)
+                    if place:
+                        total = total + half[p]
+                    if place == vn - 1:
+                        total = total.astype(BF16).astype(F32)
+                    half[p] = total
 
         for p in range(pairs):
             for h in range(ml // LANES):
@@ -181,7 +200,7 @@
 
                 def contract(v, other, p=p, cols=cols, ahead=ahead):
                     here = pl.ds(pl.multiple_of(v * nvec, nvec), nvec)
-                    line = half[p, v, :, cols]
+                    line = half[p, pl.ds(pl.multiple_of(v * valence, valence), valence), cols]
                     mine = proj[dest[2 * p], here, cols]
                     sums, kept = [], []
                     for u in range(valence):
@@ -263,7 +282,7 @@
                 out[n, k : k + 1, h * LANES : (h + 1) * LANES] = filtered[at : at + 1]
 
     drain(orb_all.at[pl.ds(0, (pn - 1) * kl)], orb_sem)
-    drain(val_all.at[pl.ds(0, vn - 1)], val_sem.at[0])
+    drain(val_all.at[pl.ds(0, vn - 1)], val_sem.at[vn])
     for a in range(2):
         drain(x_all.at[a, pl.ds(0, count - 1)], x_sem.at[0, a])
         drain(dens_all.at[a, pl.ds(0, vn - 1)], dens_sem.at[0, a])
@@ -284,20 +303,21 @@
     return pl.pallas_call(
         functools.partial(kernel, pn, vn),
         out_shape=jax.ShapeDtypeStruct(trial.shape, F32),
-        in_specs=[vmem, vmem, vmem, vmem, pl.BlockSpec(memory_space=pl.ANY), smem, smem, smem, smem],
+        in_specs=[vmem, vmem, vmem] + [pl.BlockSpec(memory_space=pl.ANY)] * 2 + [smem, smem, smem, smem],
         out_specs=vmem,
         scratch_shapes=[
             pltpu.VMEM((ktot, bands, ml), BF16),
             pltpu.VMEM((2, count) + tile, F32),
             pltpu.VMEM((2,) + tile, F32),
-            pltpu.VMEM((nvec, width), F32),
+            pltpu.VMEM((2 * kl, nvec, width), F32),
             pltpu.VMEM(tile, F32),
             pltpu.VMEM(tile, F32),
             pltpu.VMEM((ktot, NV * nvec, ml), F32),
             pltpu.VMEM((2 * pairs, NV, ml), BF16),
             pltpu.VMEM((vn, 2 * pairs, NV, ml), BF16),
-            pltpu.VMEM((pairs, NV * NV, vn * ml), BF16),
-            pltpu.VMEM((pairs, NV, NV, ml), F32),
+            pltpu.VMEM((pairs, NV * NV, ml), BF16),
+            pltpu.VMEM((pairs, NV * NV, ml), F32),
+            pltpu.VMEM(screened.shape, BF16),
             pltpu.VMEM((2, nvec, ml), F32),
             pltpu.VMEM((2, vn, nvec, ml), F32),
             pltpu.VMEM((ml, vn * ml), BF16),
@@ -306,7 +326,7 @@
             pltpu.VMEM((kl, nvec, width), F32),
             pltpu.VMEM((2, count) + tile, F32),
             pltpu.VMEM((2, count) + tile, F32),
-            dma, dma, dma((pn,)), dma((2,)), dma((2, 2)), dma((2, 2)), dma((2, 2)),
+            dma, dma, dma, dma((pn,)), dma((vn + 1,)), dma((2, 2)), dma((2, 2)), dma((2, 2)),
         ],
         compiler_params=pltpu.CompilerParams(
             collective_id=0, has_side_effects=True, vmem_limit_bytes=56 * 2**20),

time: 45.7 us -> 44.2 us (0.967)
  Pallas kernels: 44.3 us -> 42.7 us
    pallas_call x1, Pallas kernels: 44.3 us -> 42.7 us  [body(): pl.pallas_call(functools.partial(kernel, pn, vn), out_shape=jax.ShapeDtyp...]
where the time goes in v3:
time: 44.2 us; the launch traced here: 44 us
  Pallas kernels  42.7 us (97%)
  local copies, waits for them, and re-layouts  1.28 us (3%)
    pallas_call x1, Pallas kernels, body(): pl.pallas_call(functools.partial(kernel, pn, vn), out_shape=jax.ShapeDtyp...  42.7 us
    unnamed x1, local copies, waits for them, and re-layouts  1.28 us

profile of v3, /device:TPU:0, one launch (start us, length us, event | category | flops | bytes accessed | tf_op | source)
XLA Modules:
  0.0 44.0 jit_solution(8095493431415489152)
XLA Ops:
  0.0 42.7 %shard_map.91 = f32[2,2,256]{2,1,0:T(2,128)} custom-call(bf16[2,32,256]{2,1,0:T(8,128)(2,1)} %orb.1, f32[2,256]{1,0:T(2,128)} %trans.1, f32[2,2,256]{2,1,0:T(2,128)} %trial.1, bf16[2,1024,256]{2,1,0:T(8,128)(2,1)} %scr_hbm.1, bf16[1024,1024]{1,0:T(8,128)(2,1)} %bare.1, f32[3]{0:T(128)} %cheb.1, s32[3]{0:T(128)} %pair_k.1, s32[3]{0:T(128)} %pair_slot.1, ...), custom_call_target="tpu_custom_call" | custom-call | tf_op jit(solution)/shard_map/pallas_call | solution.py:303
  42.7 1.3 %copy.11 = f32[2,2,256]{2,1,0:T(2,128)} copy(f32[2,2,256]{2,1,0:T(2,128)} %shard_map.91) | data formatting | bytes 8192
